TPU v7x, 256 devices: a whole 4x4x8 slice. The times are simulated.
256 devices in a mesh: gx: 64 (over y, z, core), gy: 4 (over x).
Axes of the slice: x: 4, y: 4, z: 8, core: 2. Of those that a mesh axis runs over, the one named last changes fastest.
Arguments:
- coupling: float32 [1024, 64, 64], P('gx'), may hold values from -20 to 1920, as said below
- vertical: float32 [1024, 64, 64], P('gx'), may hold values from -10 to 21, as said below
- source: float32 [1024, 512, 64], P('gx', 'gy'), may hold values from -60 to 60
- previous: float32 [1024, 512, 64], P('gx', 'gy'), may hold values from -24 to 24
- spread_rate: float32 [64], replicated, may hold values from 0.5 to 2
Outputs:
- updated: float32 [1024, 512, 64], P('gx', 'gy')
Inputs may be any that keep to these rules, and one draw needn't show every extreme that they name: `coupling`: each block is symmetric positive definite. `vertical`: each block is symmetric, tridiagonal and positive definite.
All inputs are finite; a program needn't handle non-finite values.
Results may differ from a plain program's by a relative error of at most 0.0015.
Values sent between devices are 32-bit elements; how exact they have to be, the bound alone decides.
A program may use at most 192 MiB of HBM per device.

v0:
```python
import jax
import jax.numpy as jnp
from jax import lax
from jax.sharding import PartitionSpec as P


def extended(shard, sides, width):
    for axis, dim in sides:
        devices, length = (lax.axis_size(axis), shard.shape[dim])
        up = [(i, (i + 1) % devices) for i in range(devices)]
        down = [(j, i) for i, j in up]
        last = lax.slice_in_dim(shard, length - width, length, axis=dim)
        initial = lax.slice_in_dim(shard, 0, width, axis=dim)
        before = lax.ppermute(last, axis, up)
        after = lax.ppermute(initial, axis, down)
        shard = jnp.concatenate([before, shard, after], axis=dim)
    return shard


def passed_along(value, axis, steps):
    count = lax.axis_size(axis)
    initial, last = (max(0, -steps), min(count, count - steps))
    return lax.ppermute(value, axis, [(source, source + steps) for source in range(initial, last)])


def product(left, right):
    return jnp.matmul(left, right, precision=lax.Precision.HIGHEST)


def solve_spd(matrix, right):
    factor = jnp.linalg.cholesky(matrix)
    return jax.scipy.linalg.cho_solve((factor, True), right)


def forward_step(running, items):
    block, link, right = items
    factor = jnp.linalg.cholesky(block - running[0])
    spread = jax.scipy.linalg.cho_solve((factor, True), link)
    partial_sol = jax.scipy.linalg.cho_solve((factor, True), right + running[1])
    return ((product(link, spread), product(link, partial_sol)), (spread, partial_sol))


def backward_step(running, items):
    spread, partial_sol = items
    value = partial_sol + product(spread, running)
    return (value, value)


def split_pack(packed, width):
    return (
        packed[..., :width],
        packed[..., width : 2 * width],
        packed[..., 2 * width : 3 * width],
        packed[..., 3 * width :],
    )


def eliminate(equations, from_left, from_right, left_valid, right_valid):
    width = equations.shape[-2]
    identity = jnp.eye(width, dtype=jnp.float32)
    diag_own, lower_own, upper_own, target_own = split_pack(equations, width)
    diag_left, lower_left, upper_left, target_left = split_pack(from_left, width)
    diag_right, lower_right, upper_right, target_right = split_pack(from_right, width)
    diag_left = jnp.where(left_valid, diag_left, identity)
    diag_right = jnp.where(right_valid, diag_right, identity)
    left_factor = -jnp.swapaxes(solve_spd(diag_left, jnp.swapaxes(lower_own, -1, -2)), -1, -2)
    right_factor = -jnp.swapaxes(solve_spd(diag_right, jnp.swapaxes(upper_own, -1, -2)), -1, -2)
    new_diag = diag_own + product(left_factor, upper_left) + product(right_factor, lower_right)
    new_lower = product(left_factor, lower_left)
    new_upper = product(right_factor, upper_right)
    new_target = (
        target_own + product(left_factor, target_left) + product(right_factor, target_right)
    )
    return jnp.concatenate([new_diag, new_lower, new_upper, new_target], axis=-1)


def local(coupling, vertical, source, previous, spread_rate):
    cell_count, row_count, width = source.shape
    padded = extended(previous, (("gy", 1),), 1)
    forcing = source + spread_rate * (padded[:, 2:] + padded[:, :-2] - 2.0 * previous)
    left_link = passed_along(coupling[cell_count - 1], "gx", 1)
    prior = jnp.concatenate([left_link[None], coupling[:-1]], axis=0)
    blocks = vertical + prior + coupling
    columns = jnp.swapaxes(forcing, 1, 2)
    inner_count = cell_count - 1
    cell_index = jnp.arange(inner_count)
    first_flag = (cell_index == 0)[:, None, None]
    last_flag = (cell_index == inner_count - 1)[:, None, None]
    left_part = jnp.where(first_flag, left_link[None], 0.0)
    right_part = jnp.where(last_flag, coupling[inner_count - 1][None], 0.0)
    stacked = jnp.concatenate([left_part, right_part, columns[:inner_count]], axis=2)
    start = (jnp.zeros((width, width), jnp.float32), jnp.zeros_like(stacked[0]))
    _, (spreads, partials) = lax.scan(
        forward_step, start, (blocks[:inner_count], coupling[:inner_count], stacked)
    )
    _, spikes = lax.scan(
        backward_step, jnp.zeros_like(stacked[0]), (spreads, partials), reverse=True
    )
    near_v = spikes[:, :, :width]
    near_w = spikes[:, :, width : 2 * width]
    near_y = spikes[:, :, 2 * width :]
    link_in = coupling[inner_count - 1]
    diag_local = blocks[cell_count - 1] - product(link_in, near_w[inner_count - 1])
    target_local = columns[cell_count - 1] + product(link_in, near_y[inner_count - 1])
    side_block = -product(left_link, near_w[0])
    outgoing = jnp.concatenate(
        [product(left_link, near_v[0]), side_block, product(left_link, near_y[0])], axis=1
    )
    incoming = passed_along(outgoing, "gx", -1)
    diag_b = diag_local - incoming[:, :width]
    upper_c = incoming[:, width : 2 * width]
    target_g = target_local + incoming[:, 2 * width :]
    lower_a = jnp.swapaxes(side_block, 0, 1)
    equations = jnp.concatenate([diag_b, lower_a, upper_c, target_g], axis=1)
    device_count = lax.axis_size("gx")
    section_count = (device_count - 1).bit_length()
    position = lax.axis_index("gx")
    for section_index in range(section_count):
        distance = 1 << section_index
        from_left = passed_along(equations, "gx", distance)
        from_right = passed_along(equations, "gx", -distance)
        equations = eliminate(
            equations,
            from_left,
            from_right,
            position >= distance,
            position + distance < device_count,
        )
    separator = solve_spd(equations[:, :width], equations[:, 3 * width :])
    separator_left = passed_along(separator, "gx", 1)
    interior = near_y + product(near_v, separator_left) + product(near_w, separator)
    solved = jnp.concatenate([interior, separator[None]], axis=0)
    return jnp.swapaxes(solved, 1, 2)


def solution(mesh):
    in_specs = (
        P("gx", None, None),
        P("gx", None, None),
        P("gx", "gy", None),
        P("gx", "gy", None),
        P(),
    )
    out_specs = P("gx", "gy", None)
    return jax.shard_map(local, mesh=mesh, in_specs=in_specs, out_specs=out_specs, check_vma=False)
```

profile of v0, /device:TPU:8, one launch (start us, length us, event | category | flops | bytes accessed | tf_op | source)
XLA Modules:
  0.0 513.7 jit_solution(16271315198352885682)
XLA Ops:
  16.7 227.0 %while.33 = (s32[]{:T(128)}, f32[64,64]{1,0:T(8,128)S(1)}, f32[64,256]{1,0:T(8,128)S(1)}, f32[15,64,64]{2,1,0:T(8,128)}, f32[15,64,256]{2,1,0:T(8,128)S(1)}, /*i...) while((s32[]{:T(128)}, f32[64,64]{1,0:T(8,128)S(1)}, ...), condition=%wide.region_3.6_spmd, body=%wide.region_0.5_spmd.sunk | while | flops 47243328 | bytes 1066611 | solution.py:93
  16.9 5.8 %cholesky.631 = f32[64,64]{1,0:T(8,128)S(1)} custom-call(f32[64,64]{1,0:T(8,128)S(1)} %fusion.305), custom_call_target="Cholesky" | custom-call | tf_op jit(solution)/shard_map/while/body/eval_jaxpr/jit(cholesky)/cholesky | solution.py:37
  24.1 4.9 custom-call.50
  32.1 5.8 %cholesky.631 = f32[64,64]{1,0:T(8,128)S(1)} custom-call(f32[64,64]{1,0:T(8,128)S(1)} %fusion.305), custom_call_target="Cholesky" | custom-call | tf_op jit(solution)/shard_map/while/body/eval_jaxpr/jit(cholesky)/cholesky | solution.py:37
  39.3 4.9 custom-call.50
  47.2 5.8 %cholesky.631 = f32[64,64]{1,0:T(8,128)S(1)} custom-call(f32[64,64]{1,0:T(8,128)S(1)} %fusion.305), custom_call_target="Cholesky" | custom-call | tf_op jit(solution)/shard_map/while/body/eval_jaxpr/jit(cholesky)/cholesky | solution.py:37
  54.4 4.9 custom-call.50
  62.3 5.8 %cholesky.631 = f32[64,64]{1,0:T(8,128)S(1)} custom-call(f32[64,64]{1,0:T(8,128)S(1)} %fusion.305), custom_call_target="Cholesky" | custom-call | tf_op jit(solution)/shard_map/while/body/eval_jaxpr/jit(cholesky)/cholesky | solution.py:37
  69.5 4.9 custom-call.50
  77.5 5.8 %cholesky.631 = f32[64,64]{1,0:T(8,128)S(1)} custom-call(f32[64,64]{1,0:T(8,128)S(1)} %fusion.305), custom_call_target="Cholesky" | custom-call | tf_op jit(solution)/shard_map/while/body/eval_jaxpr/jit(cholesky)/cholesky | solution.py:37
  84.7 4.9 custom-call.50
  92.6 5.8 %cholesky.631 = f32[64,64]{1,0:T(8,128)S(1)} custom-call(f32[64,64]{1,0:T(8,128)S(1)} %fusion.305), custom_call_target="Cholesky" | custom-call | tf_op jit(solution)/shard_map/while/body/eval_jaxpr/jit(cholesky)/cholesky | solution.py:37
  99.8 4.9 custom-call.50
  107.7 5.8 %cholesky.631 = f32[64,64]{1,0:T(8,128)S(1)} custom-call(f32[64,64]{1,0:T(8,128)S(1)} %fusion.305), custom_call_target="Cholesky" | custom-call | tf_op jit(solution)/shard_map/while/body/eval_jaxpr/jit(cholesky)/cholesky | solution.py:37
  114.9 4.9 custom-call.50
  122.9 5.8 %cholesky.631 = f32[64,64]{1,0:T(8,128)S(1)} custom-call(f32[64,64]{1,0:T(8,128)S(1)} %fusion.305), custom_call_target="Cholesky" | custom-call | tf_op jit(solution)/shard_map/while/body/eval_jaxpr/jit(cholesky)/cholesky | solution.py:37
  130.1 4.9 custom-call.50
  138.0 5.8 %cholesky.631 = f32[64,64]{1,0:T(8,128)S(1)} custom-call(f32[64,64]{1,0:T(8,128)S(1)} %fusion.305), custom_call_target="Cholesky" | custom-call | tf_op jit(solution)/shard_map/while/body/eval_jaxpr/jit(cholesky)/cholesky | solution.py:37
  145.2 4.9 custom-call.50
  153.1 5.8 %cholesky.631 = f32[64,64]{1,0:T(8,128)S(1)} custom-call(f32[64,64]{1,0:T(8,128)S(1)} %fusion.305), custom_call_target="Cholesky" | custom-call | tf_op jit(solution)/shard_map/while/body/eval_jaxpr/jit(cholesky)/cholesky | solution.py:37
  160.3 4.9 custom-call.50
  168.3 5.8 %cholesky.631 = f32[64,64]{1,0:T(8,128)S(1)} custom-call(f32[64,64]{1,0:T(8,128)S(1)} %fusion.305), custom_call_target="Cholesky" | custom-call | tf_op jit(solution)/shard_map/while/body/eval_jaxpr/jit(cholesky)/cholesky | solution.py:37
  175.5 4.9 custom-call.50
  183.4 5.8 %cholesky.631 = f32[64,64]{1,0:T(8,128)S(1)} custom-call(f32[64,64]{1,0:T(8,128)S(1)} %fusion.305), custom_call_target="Cholesky" | custom-call | tf_op jit(solution)/shard_map/while/body/eval_jaxpr/jit(cholesky)/cholesky | solution.py:37
  190.6 4.9 custom-call.50
  198.5 5.8 %cholesky.631 = f32[64,64]{1,0:T(8,128)S(1)} custom-call(f32[64,64]{1,0:T(8,128)S(1)} %fusion.305), custom_call_target="Cholesky" | custom-call | tf_op jit(solution)/shard_map/while/body/eval_jaxpr/jit(cholesky)/cholesky | solution.py:37
  205.7 4.9 custom-call.50
  213.7 5.8 %cholesky.631 = f32[64,64]{1,0:T(8,128)S(1)} custom-call(f32[64,64]{1,0:T(8,128)S(1)} %fusion.305), custom_call_target="Cholesky" | custom-call | tf_op jit(solution)/shard_map/while/body/eval_jaxpr/jit(cholesky)/cholesky | solution.py:37
  220.9 4.9 custom-call.50
  228.8 5.8 %cholesky.631 = f32[64,64]{1,0:T(8,128)S(1)} custom-call(f32[64,64]{1,0:T(8,128)S(1)} %fusion.305), custom_call_target="Cholesky" | custom-call | tf_op jit(solution)/shard_map/while/body/eval_jaxpr/jit(cholesky)/cholesky | solution.py:37
  236.0 4.9 custom-call.50
  243.9 15.0 %while.34 = (s32[]{:T(128)}, f32[64,256]{1,0:T(8,128)S(1)}, f32[15,64,256]{2,1,0:T(8,128)S(1)}, f32[15,64,256]{2,1,0:T(8,128)S(1)}, f32[15,64,64]{2,1,0:T(8,128)}, /*index=5*/s32[]{:T(128)}, s32[]{:T(128)}, s32[]{:T(128)}) while((s32[]{:T(128)}, f32[64,256]{1,0:T(8,128)S(1)}, f32[15,64,256]{2,1,0:T(8,128)S(1)}, ...), condition=%wide.region_5.8_spmd.clone, body=%wide.region_4.7_spmd.clone.sunk | while | flops 12615684 | bytes 427626 | solution.py:96
  259.8 6.6 %collective-permute-start.3 = (f32[64,256]{0,1:T(8,128)S(1)}, f32[64,256]{0,1:T(8,128)S(1)}, u32[]{:S(2)}, u32[]{:S(2)}) collective-permute-start(f32[64,256]{0,1:T(8,128)S(1)} %pad_maximum_fusion.9), channel_id=1, source_target_pairs={{4,0},{8,4},{12,8},{16,12},{20,16},{24,20},{28,24},{32,28},{36,32}... | collective-permute-start | bytes 196616 | tf_op jit(solution)/shard_map/ppermute | solution.py:23
  271.2 5.9 %collective-permute-start.5 = (f32[64,320]{0,1:T(8,128)S(1)}, f32[64,320]{0,1:T(8,128)S(1)}, u32[]{:S(2)}, u32[]{:S(2)}) collective-permute-start(f32[64,320]{0,1:T(8,128)S(1)} %pad_maximum_fusion.3), channel_id=1, source_target_pairs={{4,0},{8,4},{12,8},{16,12},{20,16},{24,20},{28,24},{32,28},{36,32}... | collective-permute-start | bytes 245768 | tf_op jit(solution)/shard_map/ppermute | solution.py:23
  280.0 5.8 %cholesky.246 = f32[64,64]{1,0:T(8,128)S(1)} custom-call(f32[64,64]{1,0:T(8,128)S(1)} %fusion.184), custom_call_target="Cholesky" | custom-call | tf_op jit(solution)/shard_map/jit(cholesky)/cholesky | solution.py:31
  287.2 4.9 custom-call.37
  292.6 5.8 %cholesky.235 = f32[64,64]{1,0:T(8,128)S(1)} custom-call(f32[64,64]{1,0:T(8,128)S(1)} %fusion.188), custom_call_target="Cholesky" | custom-call | tf_op jit(solution)/shard_map/jit(cholesky)/cholesky | solution.py:31
  299.8 4.9 custom-call.36
  313.9 5.8 %cholesky.268 = f32[64,64]{1,0:T(8,128)S(1)} custom-call(f32[64,64]{1,0:T(8,128)S(1)} %fusion.174), custom_call_target="Cholesky" | custom-call | tf_op jit(solution)/shard_map/jit(cholesky)/cholesky | solution.py:31
  321.1 4.9 custom-call.39
  326.5 5.8 %cholesky.257 = f32[64,64]{1,0:T(8,128)S(1)} custom-call(f32[64,64]{1,0:T(8,128)S(1)} %fusion.179), custom_call_target="Cholesky" | custom-call | tf_op jit(solution)/shard_map/jit(cholesky)/cholesky | solution.py:31
  333.7 4.9 custom-call.38
  352.1 5.8 %cholesky.290 = f32[64,64]{1,0:T(8,128)S(1)} custom-call(f32[64,64]{1,0:T(8,128)S(1)} %fusion.164), custom_call_target="Cholesky" | custom-call | tf_op jit(solution)/shard_map/jit(cholesky)/cholesky | solution.py:31
  359.3 4.9 custom-call.41
  364.7 5.8 %cholesky.279 = f32[64,64]{1,0:T(8,128)S(1)} custom-call(f32[64,64]{1,0:T(8,128)S(1)} %fusion.169), custom_call_target="Cholesky" | custom-call | tf_op jit(solution)/shard_map/jit(cholesky)/cholesky | solution.py:31
  371.9 4.9 custom-call.40
  378.6 7.3 %collective-permute-start.11 = (f32[64,320]{0,1:T(8,128)S(1)}, f32[64,320]{0,1:T(8,128)S(1)}, u32[]{:S(2)}, u32[]{:S(2)}) collective-permute-start(f32[64,320]{0,1:T(8,128)S(1)} %pad_maximum_fusion.6), channel_id=1, source_target_pairs={{32,0},{36,4},{40,8},{44,12},{48,16},{52,20},{56,24},{60,28},{64,3... | collective-permute-start | bytes 245768 | tf_op jit(solution)/shard_map/ppermute | solution.py:23
  388.4 7.9 %collective-permute-done.11 = f32[64,320]{0,1:T(8,128)S(1)} collective-permute-done((f32[64,320]{0,1:T(8,128)S(1)}, f32[64,320]{0,1:T(8,128)S(1)}, u32[]{:S(2)}, u32[]{:S(2)}) %collective-permute-start.11) | collective-permute-done | bytes 81952 | tf_op jit(solution)/shard_map/ppermute | solution.py:23
  396.4 5.8 %cholesky.312 = f32[64,64]{1,0:T(8,128)S(1)} custom-call(f32[64,64]{1,0:T(8,128)S(1)} %fusion.154), custom_call_target="Cholesky" | custom-call | tf_op jit(solution)/shard_map/jit(cholesky)/cholesky | solution.py:31
  403.6 4.9 custom-call.43
  409.1 5.8 %cholesky.301 = f32[64,64]{1,0:T(8,128)S(1)} custom-call(f32[64,64]{1,0:T(8,128)S(1)} %fusion.159), custom_call_target="Cholesky" | custom-call | tf_op jit(solution)/shard_map/jit(cholesky)/cholesky | solution.py:31
  416.3 4.9 custom-call.42
  430.3 5.8 %cholesky.334 = f32[64,64]{1,0:T(8,128)S(1)} custom-call(f32[64,64]{1,0:T(8,128)S(1)} %fusion.144), custom_call_target="Cholesky" | custom-call | tf_op jit(solution)/shard_map/jit(cholesky)/cholesky | solution.py:31
  437.5 4.9 custom-call.45
  443.0 5.8 %cholesky.323 = f32[64,64]{1,0:T(8,128)S(1)} custom-call(f32[64,64]{1,0:T(8,128)S(1)} %fusion.149), custom_call_target="Cholesky" | custom-call | tf_op jit(solution)/shard_map/jit(cholesky)/cholesky | solution.py:31
  450.2 4.9 custom-call.44
  458.2 6.1 %collective-permute-start.14 = (f32[64,320]{0,1:T(8,128)S(1)}, f32[64,320]{0,1:T(8,128)S(1)}, u32[]{:S(2)}, u32[]{:S(2)}) collective-permute-start(f32[64,320]{0,1:T(8,128)S(1)} %pad_maximum_fusion.8), channel_id=1, source_target_pairs={{0,128},{4,132},{8,136},{12,140},{16,144},{20,148},{24,152},{28,15... | collective-permute-start | bytes 245768 | tf_op jit(solution)/shard_map/ppermute | solution.py:23
  465.8 5.8 %cholesky.356 = f32[64,64]{1,0:T(8,128)S(1)} custom-call(f32[64,64]{1,0:T(8,128)S(1)} %fusion.134), custom_call_target="Cholesky" | custom-call | tf_op jit(solution)/shard_map/jit(cholesky)/cholesky | solution.py:31
  472.9 4.9 custom-call.47
  478.4 5.8 %cholesky.345 = f32[64,64]{1,0:T(8,128)S(1)} custom-call(f32[64,64]{1,0:T(8,128)S(1)} %fusion.139), custom_call_target="Cholesky" | custom-call | tf_op jit(solution)/shard_map/jit(cholesky)/cholesky | solution.py:31
  485.6 4.9 custom-call.46
  491.3 5.8 %cholesky.367 = f32[64,64]{1,0:T(8,128)S(1)} custom-call(f32[64,64]{1,0:T(8,128)S(1)} %fusion.129), custom_call_target="Cholesky" | custom-call | tf_op jit(solution)/shard_map/jit(cholesky)/cholesky | solution.py:31
  498.5 4.9 custom-call.21
  506.8 5.2 %collective-permute-done.16 = f32[64,128]{1,0:T(8,128)S(1)} collective-permute-done((f32[64,128]{1,0:T(8,128)S(1)}, f32[64,128]{1,0:T(8,128)S(1)}, u32[]{:S(2)}, u32[]{:S(2)}) %collective-permute-start.16) | collective-permute-done | bytes 32800 | tf_op jit(solution)/shard_map/ppermute | solution.py:23
  (456 shorter events, 170.4 us)
Async XLA Ops:
  0.0 4.3 copy-start.4
  0.0 6.8 %copy-start.5 = (f32[16,128,64]{1,2,0:T(8,128)S(1)}, f32[16,128,64]{1,2,0:T(8,128)}, u32[]{:S(2)}) copy-start(f32[16,128,64]{1,2,0:T(8,128)} %param.14) | copy-start | bytes 1572868
  1.5 8.7 %collective-permute-start.1 = (f32[16,1,64]{2,1,0:T(1,128)S(1)}, f32[16,1,64]{2,1,0:T(1,128)S(1)}, u32[]{:S(2)}, u32[]{:S(2)}) collective-permute-start(f32[16,1,64]{2,1,0:T(1,128)S(1)} %get-tuple-element.222), channel_id=1, source_target_pairs={{1,0},{2,1},{3,2},{0,3},{5,4},{6,5},{7,6},{4,7},{9,8},{10,9},{11,1... | collective-permute-start | bytes 12296 | tf_op jit(solution)/shard_map/ppermute | solution.py:15
  4.3 5.8 %collective-permute-start.2 = (f32[16,1,64]{2,1,0:T(1,128)S(1)}, f32[16,1,64]{2,1,0:T(1,128)S(1)}, u32[]{:S(2)}, u32[]{:S(2)}) collective-permute-start(f32[16,1,64]{2,1,0:T(1,128)S(1)} %get-tuple-element.223), channel_id=1, source_target_pairs={{0,1},{1,2},{2,3},{3,0},{4,5},{5,6},{6,7},{7,4},{8,9},{9,10},{10,1... | collective-permute-start | bytes 12296 | tf_op jit(solution)/shard_map/ppermute | solution.py:14
  4.6 8.4 %collective-permute-start = (f32[64,64]{0,1:T(8,128)S(1)}, f32[64,64]{0,1:T(8,128)S(1)}, u32[]{:S(2)}, u32[]{:S(2)}) collective-permute-start(f32[64,64]{0,1:T(8,128)S(1)} %slice_bitcast_fusion.2), channel_id=1, source_target_pairs={{0,4},{4,8},{8,12},{12,16},{16,20},{20,24},{24,28},{28,32},{32,36}... | collective-permute-start | bytes 49160 | tf_op jit(solution)/shard_map/ppermute | solution.py:23
  6.6 3.6 copy-start.6
  11.8 1.2 copy-start
  13.0 0.6 copy-start.1
  13.9 1.6 copy-start.2
  243.8 15.1 %copy-start.3 = (f32[64,64]{0,1:T(8,128)S(1)}, f32[64,64]{0,1:T(8,128)}, u32[]{:S(2)}) copy-start(f32[64,64]{0,1:T(8,128)} %copy-done.1) | copy-start | bytes 49156
  259.8 9.1 %collective-permute-start.3 = (f32[64,256]{0,1:T(8,128)S(1)}, f32[64,256]{0,1:T(8,128)S(1)}, u32[]{:S(2)}, u32[]{:S(2)}) collective-permute-start(f32[64,256]{0,1:T(8,128)S(1)} %pad_maximum_fusion.9), channel_id=1, source_target_pairs={{4,0},{8,4},{12,8},{16,12},{20,16},{24,20},{28,24},{32,28},{36,32}... | collective-permute-start | bytes 196616 | tf_op jit(solution)/shard_map/ppermute | solution.py:23
  271.2 8.7 %collective-permute-start.5 = (f32[64,320]{0,1:T(8,128)S(1)}, f32[64,320]{0,1:T(8,128)S(1)}, u32[]{:S(2)}, u32[]{:S(2)}) collective-permute-start(f32[64,320]{0,1:T(8,128)S(1)} %pad_maximum_fusion.3), channel_id=1, source_target_pairs={{4,0},{8,4},{12,8},{16,12},{20,16},{24,20},{28,24},{32,28},{36,32}... | collective-permute-start | bytes 245768 | tf_op jit(solution)/shard_map/ppermute | solution.py:23
  277.1 15.4 %collective-permute-start.4 = (f32[64,320]{0,1:T(8,128)S(1)}, f32[64,320]{0,1:T(8,128)S(1)}, u32[]{:S(2)}, u32[]{:S(2)}) collective-permute-start(f32[64,320]{0,1:T(8,128)S(1)} %pad_maximum_fusion.3), channel_id=1, source_target_pairs={{0,4},{4,8},{8,12},{12,16},{16,20},{20,24},{24,28},{28,32},{32,36}... | collective-permute-start | bytes 245768 | tf_op jit(solution)/shard_map/ppermute | solution.py:23
  306.6 7.2 %collective-permute-start.7 = (f32[64,320]{0,1:T(8,128)S(1)}, f32[64,320]{0,1:T(8,128)S(1)}, u32[]{:S(2)}, u32[]{:S(2)}) collective-permute-start(f32[64,320]{0,1:T(8,128)S(1)} %pad_maximum_fusion.4), channel_id=1, source_target_pairs={{8,0},{12,4},{16,8},{20,12},{24,16},{28,20},{32,24},{36,28},{40,32... | collective-permute-start | bytes 245768 | tf_op jit(solution)/shard_map/ppermute | solution.py:23
  309.0 17.4 %collective-permute-start.6 = (f32[64,320]{0,1:T(8,128)S(1)}, f32[64,320]{0,1:T(8,128)S(1)}, u32[]{:S(2)}, u32[]{:S(2)}) collective-permute-start(f32[64,320]{0,1:T(8,128)S(1)} %pad_maximum_fusion.4), channel_id=1, source_target_pairs={{0,8},{4,12},{8,16},{12,20},{16,24},{20,28},{24,32},{28,36},{32,40... | collective-permute-start | bytes 245768 | tf_op jit(solution)/shard_map/ppermute | solution.py:23
  340.5 11.5 %collective-permute-start.9 = (f32[64,320]{0,1:T(8,128)S(1)}, f32[64,320]{0,1:T(8,128)S(1)}, u32[]{:S(2)}, u32[]{:S(2)}) collective-permute-start(f32[64,320]{0,1:T(8,128)S(1)} %pad_maximum_fusion.5), channel_id=1, source_target_pairs={{16,0},{20,4},{24,8},{28,12},{32,16},{36,20},{40,24},{44,28},{48,3... | collective-permute-start | bytes 245768 | tf_op jit(solution)/shard_map/ppermute | solution.py:23
  343.3 21.3 %collective-permute-start.8 = (f32[64,320]{0,1:T(8,128)S(1)}, f32[64,320]{0,1:T(8,128)S(1)}, u32[]{:S(2)}, u32[]{:S(2)}) collective-permute-start(f32[64,320]{0,1:T(8,128)S(1)} %pad_maximum_fusion.5), channel_id=1, source_target_pairs={{0,16},{4,20},{8,24},{12,28},{16,32},{20,36},{24,40},{28,44},{32,4... | collective-permute-start | bytes 245768 | tf_op jit(solution)/shard_map/ppermute | solution.py:23
  378.6 17.7 %collective-permute-start.11 = (f32[64,320]{0,1:T(8,128)S(1)}, f32[64,320]{0,1:T(8,128)S(1)}, u32[]{:S(2)}, u32[]{:S(2)}) collective-permute-start(f32[64,320]{0,1:T(8,128)S(1)} %pad_maximum_fusion.6), channel_id=1, source_target_pairs={{32,0},{36,4},{40,8},{44,12},{48,16},{52,20},{56,24},{60,28},{64,3... | collective-permute-start | bytes 245768 | tf_op jit(solution)/shard_map/ppermute | solution.py:23
  386.0 23.0 %collective-permute-start.10 = (f32[64,320]{0,1:T(8,128)S(1)}, f32[64,320]{0,1:T(8,128)S(1)}, u32[]{:S(2)}, u32[]{:S(2)}) collective-permute-start(f32[64,320]{0,1:T(8,128)S(1)} %pad_maximum_fusion.6), channel_id=1, source_target_pairs={{0,32},{4,36},{8,40},{12,44},{16,48},{20,52},{24,56},{28,60},{32,6... | collective-permute-start | bytes 245768 | tf_op jit(solution)/shard_map/ppermute | solution.py:23
  423.0 7.2 %collective-permute-start.13 = (f32[64,320]{0,1:T(8,128)S(1)}, f32[64,320]{0,1:T(8,128)S(1)}, u32[]{:S(2)}, u32[]{:S(2)}) collective-permute-start(f32[64,320]{0,1:T(8,128)S(1)} %pad_maximum_fusion.7), channel_id=1, source_target_pairs={{64,0},{68,4},{72,8},{76,12},{80,16},{84,20},{88,24},{92,28},{96,3... | collective-permute-start | bytes 245768 | tf_op jit(solution)/shard_map/ppermute | solution.py:23
  425.0 17.9 %collective-permute-start.12 = (f32[64,320]{0,1:T(8,128)S(1)}, f32[64,320]{0,1:T(8,128)S(1)}, u32[]{:S(2)}, u32[]{:S(2)}) collective-permute-start(f32[64,320]{0,1:T(8,128)S(1)} %pad_maximum_fusion.7), channel_id=1, source_target_pairs={{0,64},{4,68},{8,72},{12,76},{16,80},{20,84},{24,88},{28,92},{32,9... | collective-permute-start | bytes 245768 | tf_op jit(solution)/shard_map/ppermute | solution.py:23
  456.9 8.7 %collective-permute-start.15 = (f32[64,320]{0,1:T(8,128)S(1)}, f32[64,320]{0,1:T(8,128)S(1)}, u32[]{:S(2)}, u32[]{:S(2)}) collective-permute-start(f32[64,320]{0,1:T(8,128)S(1)} %pad_maximum_fusion.8), channel_id=1, source_target_pairs={{128,0},{132,4},{136,8},{140,12},{144,16},{148,20},{152,24},{156,2... | collective-permute-start | bytes 245768 | tf_op jit(solution)/shard_map/ppermute | solution.py:23
  458.2 20.0 %collective-permute-start.14 = (f32[64,320]{0,1:T(8,128)S(1)}, f32[64,320]{0,1:T(8,128)S(1)}, u32[]{:S(2)}, u32[]{:S(2)}) collective-permute-start(f32[64,320]{0,1:T(8,128)S(1)} %pad_maximum_fusion.8), channel_id=1, source_target_pairs={{0,128},{4,132},{8,136},{12,140},{16,144},{20,148},{24,152},{28,15... | collective-permute-start | bytes 245768 | tf_op jit(solution)/shard_map/ppermute | solution.py:23
  504.3 7.7 %collective-permute-start.16 = (f32[64,128]{1,0:T(8,128)S(1)}, f32[64,128]{1,0:T(8,128)S(1)}, u32[]{:S(2)}, u32[]{:S(2)}) collective-permute-start(f32[64,128]{1,0:T(8,128)S(1)} %fusion.125), channel_id=1, source_target_pairs={{0,4},{4,8},{8,12},{12,16},{16,20},{20,24},{24,28},{28,32},{32,36}... | collective-permute-start | bytes 98312 | tf_op jit(solution)/shard_map/ppermute | solution.py:23
where the time goes:
time: 522 us; the launch traced here: 514 us
  other arithmetic  343 us (66%)
  matrix products  72.8 us (14%)
  starting transfers between devices  57.5 us (11%)
  waiting for transfers between devices  25.5 us (5%)
  local copies, waits for them, and re-layouts  11.8 us (2%)
    another operation x45, other arithmetic, forward_step(): factor = jnp.linalg.cholesky(block - running[0])  97.8 us
    another operation x39, other arithmetic, solve_spd(): factor = jnp.linalg.cholesky(matrix)  84.7 us
    another operation x30, other arithmetic, forward_step(): spread = jax.scipy.linalg.cho_solve((factor, True), link)  83.2 us
    another operation x26, other arithmetic, solve_spd(): return jax.scipy.linalg.cho_solve((factor, True), right)  72.1 us
    ppermute x15, starting transfers between devices, passed_along(): lax.ppermute(value, axis, [(source, source + steps) for source in range(i...  54.6 us
    dot_general x86, matrix products, product(): return jnp.matmul(left, right, precision=lax.Precision.HIGHEST)  32.8 us
    ppermute x15, waiting for transfers between devices, passed_along(): lax.ppermute(value, axis, [(source, source + steps) for source in range(i...  25.5 us
    another operation x30, matrix products, forward_step(): partial_sol = jax.scipy.linalg.cho_solve((factor, True), right + running[1])  19.5 us
  transfers between devices with their start and end apart: 17, of which 9 were waited for; matrix products, arithmetic and copies ran while one was open for 16% of the time, Pallas kernels for 0%

commit v1 on v0

v1 whole, which is shorter than its diff:
```python
import jax
import jax.numpy as jnp
from jax import lax
from jax.experimental import pallas as pl
from jax.experimental.pallas import tpu as pltpu
from jax.sharding import PartitionSpec as P

CELLS = 16
ROWS = 128
W = 64
CHIPS_Z = 8
CHIPS_Y = 4
CHIPS_X = 4
MESH = pl.DeviceIdType.MESH


def dot(left, right, left_dim=1):
    return lax.dot_general(
        left,
        right,
        (((left_dim,), (0,)), ((), ())),
        precision=lax.Precision.HIGHEST,
        preferred_element_type=jnp.float32,
    )


def iota(shape, dim):
    return lax.broadcasted_iota(jnp.int32, shape, dim)


def lane_copy(value, lane):
    return jnp.broadcast_to(lax.slice_in_dim(value, lane, lane + 1, axis=2), value.shape)


def inverse(augmented):
    sub = iota((1, 8, 128), 1)

    def block(_, value):
        columns = [lane_copy(value, j) for j in range(8)]
        turned = pltpu.roll(value, 120, 2)
        top = turned[:, :8]
        head = [column[:, :8] for column in columns]
        recip = 1.0 / head[0][:, 0:1]
        for j in range(8):
            next_recip = None
            if j < 7:
                cross = head[j][:, j + 1 : j + 2] * head[j + 1][:, j : j + 1]
                next_recip = 1.0 / (head[j + 1][:, j + 1 : j + 2] - cross * recip)
            row = top[:, j : j + 1] * recip
            for k in range(j + 1, 8):
                entry = head[k][:, j : j + 1] * recip
                head[k] = jnp.where(sub == j, entry, head[k] - head[j] * entry)
            top = jnp.where(sub == j, row, top - head[j] * row)
            recip = next_recip
        terms = [columns[j][:, 8:] * top[:, j : j + 1] for j in range(8)]
        total = ((terms[0] + terms[1]) + (terms[2] + terms[3])) + (
            (terms[4] + terms[5]) + (terms[6] + terms[7])
        )
        return jnp.concatenate([turned[:, 8:] - total, top], axis=1)

    return lax.fori_loop(0, 8, block, augmented)


def augmented(link_excess, left):
    lane = iota((W, 128), 1)
    eye = (lane == iota((W, 128), 0) + W).astype(jnp.float32)
    value = link_excess + pltpu.roll(link_excess, W, 1)
    if left is not None:
        value = value + jnp.concatenate([left, left], axis=0).T[:W]
    return jnp.where(lane < W, value, eye)


def reduce_nodes(nodes, ghost, solved, count):
    lane = iota((W, 128), 1)
    stride = 1
    while stride < count:
        picks = range(stride, count, 2 * stride)
        inverses = inverse(
            jnp.stack([augmented(nodes[i, 0], nodes[i - stride, 0]) for i in picks])
        )
        for at, i in enumerate(picks):
            both = jnp.concatenate([nodes[i, 0], nodes[i, 1]], axis=1)
            answer = dot(inverses[at][:, :W], both)
            solved[i, 0] = answer[:, :128]
            solved[i, 1] = answer[:, 128:]
            before = nodes[i - stride, 0]
            to_left = dot(before[:, :W], answer)
            nodes[i - stride, 0] = jnp.where(lane < W, 0.0, before) + to_left[:, :128]
            nodes[i - stride, 1] = nodes[i - stride, 1] + to_left[:, 128:]
            to_right = dot(nodes[i, 0][:, :W], answer, 0)
            excess = jnp.where(lane < W, 0.0, to_right[:, :128])
            if i + stride < count:
                nodes[i + stride, 0] = nodes[i + stride, 0] + excess
                nodes[i + stride, 1] = nodes[i + stride, 1] + to_right[:, 128:]
            elif ghost is not None:
                ghost[0] = ghost[0] + excess
                ghost[1] = ghost[1] + to_right[:, 128:]
        stride *= 2


def expand_nodes(solved, field, count):
    stride = count // 2
    while stride >= 1:
        for i in range(stride, count, 2 * stride):
            before, after = field[i - stride], field[i + stride]
            change = jnp.concatenate([after - before, -before], axis=0)
            field[i] = solved[i, 1] + before + dot(solved[i, 0], change)
        stride //= 2


def chain(slots, nodes, ghost, count):
    lane = iota((W, 128), 1)
    for i in range(count):
        if i == 0:
            nodes[0] = slots[0, 0:2]
        else:
            nodes[i, 0] = slots[i, 0] + jnp.where(lane < W, 0.0, slots[i - 1, 2])
            nodes[i, 1] = slots[i, 1] + slots[i - 1, 3]
    if ghost is not None:
        ghost[...] = slots[count - 1, 2:4]


def kernel(
    coupling,
    vertical,
    source,
    previous,
    rate,
    out,
    edge_out,
    edge_in,
    nodes,
    ghost,
    solved,
    field,
    pair_slots,
    pair_nodes,
    pair_ghost,
    pair_solved,
    pair_field,
    z_slots,
    z_nodes,
    z_ghost,
    z_solved,
    z_field,
    y_slots,
    y_nodes,
    y_solved,
    y_field,
    edge_send,
    edge_recv,
    pair_send,
    pair_recv,
    z_send,
    z_recv,
    y_send,
    y_recv,
):
    gx, gy = lax.axis_index("gx"), lax.axis_index("gy")
    core = lax.rem(gx, 2)
    chip = lax.div(gx, 2)
    z = lax.rem(chip, CHIPS_Z)
    y = lax.div(chip, CHIPS_Z)

    def at(y_, z_, core_):
        return (y_ * CHIPS_Z + z_) * 2 + core_

    x_up = (gx, lax.rem(gy + 1, CHIPS_X))
    x_down = (gx, lax.rem(gy + CHIPS_X - 1, CHIPS_X))
    partner = (at(y, z, 1 - core), gy)
    z_to = [(at(y, lax.rem(z + d, CHIPS_Z), core), gy) for d in range(1, CHIPS_Z)]
    y_to = [(at(lax.rem(y + d, CHIPS_Y), z, core), gy) for d in range(1, CHIPS_Y)]

    barrier = pltpu.get_barrier_semaphore()
    everyone = [x_up, x_down, partner] + z_to + y_to
    for peer in everyone:
        pl.semaphore_signal(barrier, inc=1, device_id=peer, device_id_type=MESH)
    edge_out[...] = jnp.zeros_like(edge_out)
    edge_out[0, :, 0:W] = previous[:, ROWS - 1, :]
    edge_out[1, :, 0:W] = previous[:, 0, :]
    pl.semaphore_wait(barrier, len(everyone))

    def remote(src, dst, send, recv, peer):
        copy = pltpu.make_async_remote_copy(
            src_ref=src,
            dst_ref=dst,
            send_sem=send,
            recv_sem=recv,
            device_id=peer,
            device_id_type=MESH,
        )
        copy.start()
        return copy

    edges = [
        remote(edge_out.at[0], edge_in.at[0], edge_send.at[0], edge_recv.at[0], x_up),
        remote(edge_out.at[1], edge_in.at[1], edge_send.at[1], edge_recv.at[1], x_down),
    ]

    lane = iota((W, 128), 1)
    for i in range(CELLS):
        nodes[i, 0, :, 0:W] = coupling[i]
        nodes[i, 0, :, W:128] = vertical[i]
    for edge in edges:
        edge.wait()
    row_index = iota((ROWS, W), 0)
    for i in range(CELLS):
        own = previous[i]
        below = jnp.where(row_index == 0, edge_in[0, i : i + 1, 0:W], pltpu.roll(own, 1, 0))
        above = jnp.where(
            row_index == ROWS - 1, edge_in[1, i : i + 1, 0:W], pltpu.roll(own, ROWS - 1, 0)
        )
        forcing = source[i] + rate[...] * (above + below - 2.0 * own)
        nodes[i, 1] = forcing.T
    ghost[...] = jnp.zeros_like(ghost)
    reduce_nodes(nodes, ghost, solved, CELLS)

    pair_slots[core, 0:2] = nodes[0]
    pair_slots[core, 2:4] = ghost[...]
    remote(
        pair_slots.at[core], pair_slots.at[core], pair_send.at[0], pair_recv.at[0], partner
    ).wait()
    chain(pair_slots, pair_nodes, pair_ghost, 2)
    reduce_nodes(pair_nodes, pair_ghost, pair_solved, 2)

    z_slots[z, 0:2] = pair_nodes[0]
    z_slots[z, 2:4] = pair_ghost[...]
    sends = [
        remote(z_slots.at[z], z_slots.at[z], z_send.at[d], z_recv.at[d], z_to[d])
        for d in range(CHIPS_Z - 1)
    ]
    for send in sends:
        send.wait()
    chain(z_slots, z_nodes, z_ghost, CHIPS_Z)
    reduce_nodes(z_nodes, z_ghost, z_solved, CHIPS_Z)

    y_slots[y, 0:2] = z_nodes[0]
    y_slots[y, 2:4] = z_ghost[...]
    sends = [
        remote(y_slots.at[y], y_slots.at[y], y_send.at[d], y_recv.at[d], y_to[d])
        for d in range(CHIPS_Y - 1)
    ]
    for send in sends:
        send.wait()
    chain(y_slots, y_nodes, None, CHIPS_Y)
    reduce_nodes(y_nodes, None, y_solved, CHIPS_Y)

    first = inverse(augmented(y_nodes[0, 0], None)[None])
    y_field[0] = dot(first[0][:, :W], y_nodes[0, 1])
    y_field[CHIPS_Y] = jnp.zeros((W, ROWS), jnp.float32)
    expand_nodes(y_solved, y_field, CHIPS_Y)
    z_field[0] = y_field[y]
    z_field[CHIPS_Z] = y_field[y + 1]
    expand_nodes(z_solved, z_field, CHIPS_Z)
    pair_field[0] = z_field[z]
    pair_field[2] = z_field[z + 1]
    expand_nodes(pair_solved, pair_field, 2)
    field[0] = pair_field[core]
    field[CELLS] = pair_field[core + 1]
    expand_nodes(solved, field, CELLS)
    for i in range(CELLS):
        out[i] = field[i].T


def local(coupling, vertical, source, previous, spread_rate):
    f32 = jnp.float32

    def vmem(*shape):
        return pltpu.VMEM(shape + (W, 128), f32)

    dma = pltpu.SemaphoreType.DMA
    return pl.pallas_call(
        kernel,
        out_shape=jax.ShapeDtypeStruct((CELLS, ROWS, W), f32),
        in_specs=[pl.BlockSpec(memory_space=pltpu.VMEM)] * 5,
        out_specs=pl.BlockSpec(memory_space=pltpu.VMEM),
        scratch_shapes=[
            pltpu.VMEM((2, CELLS, 128), f32),
            pltpu.VMEM((2, CELLS, 128), f32),
            vmem(CELLS, 2),
            vmem(2),
            vmem(CELLS, 2),
            vmem(CELLS + 1),
            vmem(2, 4),
            vmem(2, 2),
            vmem(2),
            vmem(2, 2),
            vmem(3),
            vmem(CHIPS_Z, 4),
            vmem(CHIPS_Z, 2),
            vmem(2),
            vmem(CHIPS_Z, 2),
            vmem(CHIPS_Z + 1),
            vmem(CHIPS_Y, 4),
            vmem(CHIPS_Y, 2),
            vmem(CHIPS_Y, 2),
            vmem(CHIPS_Y + 1),
            dma((2,)),
            dma((2,)),
            dma((1,)),
            dma((1,)),
            dma((CHIPS_Z - 1,)),
            dma((CHIPS_Z - 1,)),
            dma((CHIPS_Y - 1,)),
            dma((CHIPS_Y - 1,)),
        ],
        compiler_params=pltpu.CompilerParams(
            collective_id=0, has_side_effects=True, vmem_limit_bytes=48 * 1024 * 1024
        ),
        cost_estimate=pl.CostEstimate(
            flops=400_000_000, bytes_accessed=4_000_000, transcendentals=0
        ),
    )(coupling, vertical, source, previous, spread_rate.reshape(1, W))


def solution(mesh):
    cells = P("gx", None, None)
    slab = P("gx", "gy", None)
    return jax.shard_map(
        local,
        mesh=mesh,
        in_specs=(cells, cells, slab, slab, P()),
        out_specs=slab,
        check_vma=False,
    )
```

time: 522 us -> 92.8 us (0.18)
  the two profiles are of different devices: /device:TPU:8 before, /device:TPU:1 now
where the time goes in v1:
time: 92.8 us; the launch traced here: 92.6 us
  Pallas kernels  87.3 us (94%)
  local copies, waits for them, and re-layouts  5.27 us (6%)
    pallas_call x1, Pallas kernels, local(): pl.pallas_call(kernel, out_shape=jax.ShapeDtypeStruct((CELLS, ROWS, W), f...  87.3 us
    unnamed x10, local copies, waits for them, and re-layouts  4.16 us

profile of v1, /device:TPU:1, one launch (start us, length us, event | category | flops | bytes accessed | tf_op | source)
XLA Modules:
  0.0 92.6 jit_solution(6154897379890112958)
XLA Ops:
  0.0 0.0 copy-start.3
  0.0 1.4 %copy.6.source = f32[16,128,64]{2,1,0:T(8,128)S(1)} copy(f32[16,128,64]{1,2,0:T(8,128)} %param.7) | data formatting | bytes 1048576 | tf_op args[2]
  1.4 0.0 copy-done.3
  1.5 0.0 copy-start.2
  1.5 0.3 copy.7.previous
  1.8 0.3 copy-done.2
  2.1 0.0 copy-start
  2.1 1.0 %copy-done = f32[16,64,64]{2,1,0:T(8,128)S(1)} copy-done((f32[16,64,64]{2,1,0:T(8,128)S(1)}, f32[16,64,64]{2,1,0:T(8,128)}, u32[]{:S(2)}) %copy-start) | copy-done | bytes 262168
  3.2 0.0 copy-start.1
  3.2 1.0 %copy-done.1 = f32[16,64,64]{2,1,0:T(8,128)S(1)} copy-done((f32[16,64,64]{2,1,0:T(8,128)S(1)}, f32[16,64,64]{2,1,0:T(8,128)}, u32[]{:S(2)}) %copy-start.1) | copy-done | bytes 262168
  4.2 87.3 %shard_map.55 = f32[16,128,64]{2,1,0:T(8,128)S(1)} custom-call(f32[16,64,64]{2,1,0:T(8,128)S(1)} %copy-done, f32[16,64,64]{2,1,0:T(8,128)S(1)} %copy-done.1, f32[16,128,64]{2,1,0:T(8,128)S(1)} %copy.6.source, f32[16,128,64]{2,1,0:T(8,128)S(1)} %copy.7.previous, f32[1,64]{1,0:T(1,128)S(1)} %bitcast.1), custom_call_target="tpu_custom_call" | custom-call | flops 400000000 | bytes 4000000 | tf_op jit(solution)/shard_map/pallas_call | solution.py:272
  91.5 1.1 %copy.8 = f32[16,128,64]{1,2,0:T(8,128)} copy(f32[16,128,64]{2,1,0:T(8,128)S(1)} %shard_map.55) | data formatting | bytes 1048576 | tf_op jit(solution)/shard_map/pallas_call | solution.py:272
Async XLA Ops:
  0.0 1.4 %copy-start.3 = (f32[16,128,64]{1,2,0:T(8,128)S(1)}, f32[16,128,64]{1,2,0:T(8,128)}, u32[]{:S(2)}) copy-start(f32[16,128,64]{1,2,0:T(8,128)} %param.8) | copy-start | bytes 1572868
  1.5 0.7 copy-start.2
  2.1 1.0 %copy-start = (f32[16,64,64]{2,1,0:T(8,128)S(1)}, f32[16,64,64]{2,1,0:T(8,128)}, u32[]{:S(2)}) copy-start(f32[16,64,64]{2,1,0:T(8,128)} %coupling.1) | copy-start | bytes 786436
  3.2 1.0 %copy-start.1 = (f32[16,64,64]{2,1,0:T(8,128)S(1)}, f32[16,64,64]{2,1,0:T(8,128)}, u32[]{:S(2)}) copy-start(f32[16,64,64]{2,1,0:T(8,128)} %vertical.1) | copy-start | bytes 786436

commit v2 on v1

v2 whole, which is shorter than its diff:
```python
import jax
import jax.numpy as jnp
from jax import lax
from jax.experimental import pallas as pl
from jax.experimental.pallas import tpu as pltpu
from jax.sharding import PartitionSpec as P

CELLS = 16
ROWS = 128
W = 64
CHIPS_Z = 8
CHIPS_Y = 4
CHIPS_X = 4
MESH = pl.DeviceIdType.MESH


def dot(left, right, left_dim=1):
    return lax.dot_general(
        left,
        right,
        (((left_dim,), (0,)), ((), ())),
        precision=lax.Precision.HIGH,
        preferred_element_type=jnp.float32,
    )


def iota(shape, dim):
    return lax.broadcasted_iota(jnp.int32, shape, dim)


def lane_copy(value, lane):
    return jnp.broadcast_to(lax.slice_in_dim(value, lane, lane + 1, axis=2), value.shape)


def inverse(augmented):
    sub = iota((1, 8, 128), 1)

    def block(_, value):
        columns = [lane_copy(value, j) for j in range(8)]
        turned = pltpu.roll(value, 120, 2)
        top = turned[:, :8]
        head = [column[:, :8] for column in columns]
        recip = 1.0 / head[0][:, 0:1]
        for j in range(8):
            next_recip = None
            if j < 7:
                cross = head[j][:, j + 1 : j + 2] * head[j + 1][:, j : j + 1]
                next_recip = 1.0 / (head[j + 1][:, j + 1 : j + 2] - cross * recip)
            row = top[:, j : j + 1] * recip
            for k in range(j + 1, 8):
                entry = head[k][:, j : j + 1] * recip
                head[k] = jnp.where(sub == j, entry, head[k] - head[j] * entry)
            top = jnp.where(sub == j, row, top - head[j] * row)
            recip = next_recip
        terms = [columns[j][:, 8:] * top[:, j : j + 1] for j in range(8)]
        total = ((terms[0] + terms[1]) + (terms[2] + terms[3])) + (
            (terms[4] + terms[5]) + (terms[6] + terms[7])
        )
        return jnp.concatenate([turned[:, 8:] - total, top], axis=1)

    return lax.fori_loop(0, 8, block, augmented)


def augmented(link_excess, left, symmetric=False):
    lane = iota((W, 128), 1)
    eye = (lane == iota((W, 128), 0) + W).astype(jnp.float32)
    value = link_excess + pltpu.roll(link_excess, W, 1)
    if left is not None:
        value = value + (left if symmetric else jnp.concatenate([left, left], axis=0).T[:W])
    return jnp.where(lane < W, value, eye)


def high_lanes(value):
    return jnp.where(iota(value.shape, 1) < W, 0.0, value)


def picks_of(stride, count):
    return range(stride, count, 2 * stride)


def strides_of(count):
    return [1 << k for k in range(count.bit_length() - 1)]


def reduce_links(links, ghost, solved, inverses, count, stride, symmetric=False):
    picks = picks_of(stride, count)
    found = inverse(
        jnp.stack([augmented(links[i], links[i - stride], symmetric) for i in picks])
    )
    for at, i in enumerate(picks):
        inverses[i] = found[at]
        answer = dot(found[at][:, :W], links[i])
        solved[i] = answer
        before = links[i - stride]
        links[i - stride] = high_lanes(before) + dot(before[:, :W], answer)
        if i + stride < count:
            links[i + stride] = links[i + stride] + high_lanes(dot(links[i][:, :W], answer, 0))
        elif ghost is not None:
            ghost[...] = ghost[...] + high_lanes(dot(links[i][:, :W], answer, 0))


def reduce_rhs(rhs, ghost, solved, inverses, count, stride):
    for i in picks_of(stride, count):
        own = rhs[i]
        passed = dot(solved[i], own, 0)
        rhs[i - stride] = rhs[i - stride] + (own - passed[:W] - passed[W:])
        if i + stride < count:
            rhs[i + stride] = rhs[i + stride] + passed[:W]
        elif ghost is not None:
            ghost[...] = ghost[...] + passed[:W]
        rhs[i] = dot(inverses[i][:, :W], own)


def expand(solved, rhs, field, count):
    for stride in reversed(strides_of(count)):
        for i in picks_of(stride, count):
            before, after = field[i - stride], field[i + stride]
            change = jnp.concatenate([after - before, -before], axis=0)
            field[i] = rhs[i] + before + dot(solved[i], change)


def packed_links(link_excess, ghost):
    low = pltpu.roll(ghost[: W // 2], W, 1)
    return jnp.concatenate([link_excess, low + high_lanes(ghost[W // 2 :])], axis=0)


def unpacked_ghost(packed):
    tail = packed[W:]
    return high_lanes(jnp.concatenate([pltpu.roll(tail, W, 1), tail], axis=0))


def chain_links(packed, links, ghost, count):
    for i in range(count):
        value = packed(i)[:W]
        if i > 0:
            value = value + unpacked_ghost(packed(i - 1))
        links[i] = value
    if ghost is not None:
        ghost[...] = unpacked_ghost(packed(count - 1))


def chain_rhs(own, passed, rhs, ghost, count):
    for i in range(count):
        rhs[i] = own(i) + passed(i - 1) if i > 0 else own(i)
    if ghost is not None:
        ghost[...] = passed(count - 1)


def kernel(coupling, vertical, source, previous, rate, out, *scratch):
    (coupling_in, vertical_in, source_in, previous_in, in_sems) = scratch[:5]
    (edge_out, edge_in, edge_send, edge_recv) = scratch[5:9]
    (links, ghost, solved, inverses, rhs, rhs_ghost, field) = scratch[9:16]
    (p_slots, p_links, p_ghost, p_solved, p_inverses) = scratch[16:21]
    (p_rslots, p_rhs, p_rhs_ghost, p_field, p_send, p_recv) = scratch[21:27]
    (z_slots, z_links, z_ghost, z_solved, z_inverses) = scratch[27:32]
    (z_rslots, z_rhs, z_rhs_ghost, z_field, z_send, z_recv, f_send, f_recv) = scratch[32:40]
    (y_slots, y_links, y_solved, y_inverses) = scratch[40:44]
    (y_rslots, y_rhs, y_field, y_send, y_recv) = scratch[44:49]

    gx, gy = lax.axis_index("gx"), lax.axis_index("gy")
    core = lax.rem(gx, 2)
    chip = lax.div(gx, 2)
    z = lax.rem(chip, CHIPS_Z)
    y = lax.div(chip, CHIPS_Z)

    def at(y_, z_, core_):
        return (y_ * CHIPS_Z + z_) * 2 + core_

    x_up = (gx, lax.rem(gy + 1, CHIPS_X))
    x_down = (gx, lax.rem(gy + CHIPS_X - 1, CHIPS_X))
    partner = (at(y, z, 1 - core), gy)
    z_to = {d: (at(y, lax.rem(z + d, CHIPS_Z), core), gy) for d in range(1, CHIPS_Z)}
    y_to = {d: (at(lax.rem(y + d, CHIPS_Y), z, core), gy) for d in range(1, CHIPS_Y)}
    z_order = (4, 3, 5, 2, 6, 1, 7)
    z_arrive = (1, 7, 2, 6, 3, 5, 4)
    y_order = (2, 1, 3)

    barrier = pltpu.get_barrier_semaphore()
    everyone = [x_up, x_down, partner] + list(z_to.values()) + list(y_to.values())
    for peer in everyone:
        pl.semaphore_signal(barrier, inc=1, device_id=peer, device_id_type=MESH)
    loads = [
        pltpu.make_async_copy(src, dst, in_sems.at[k])
        for k, (src, dst) in enumerate(
            [
                (coupling, coupling_in),
                (vertical, vertical_in),
                (previous, previous_in),
                (source, source_in),
            ]
        )
    ]
    for load in loads:
        load.start()

    def remote(src, dst, send, recv, peer):
        copy = pltpu.make_async_remote_copy(
            src_ref=src,
            dst_ref=dst,
            send_sem=send,
            recv_sem=recv,
            device_id=peer,
            device_id_type=MESH,
        )
        copy.start()
        return copy

    lane = iota((W, 128), 1)
    loads[0].wait()
    loads[1].wait()
    for i in range(CELLS):
        links[i, :, 0:W] = coupling_in[i]
        links[i, :, W:128] = vertical_in[i]
    ghost[...] = jnp.zeros_like(ghost)
    reduce_links(links, ghost, solved, inverses, CELLS, 1, True)

    loads[2].wait()
    edges_value = jnp.zeros((W, 128), jnp.float32)
    for i in range(CELLS):
        own = previous_in[i]
        edges_value = jnp.where(lane == i, pltpu.roll(own, i + 1, 1), edges_value)
        edges_value = jnp.where(lane == W + i, pltpu.roll(own, W + i, 1), edges_value)
    edge_out[...] = edges_value
    pl.semaphore_wait(barrier, len(everyone))
    edges = [
        remote(edge_out, edge_in.at[0], edge_send.at[0], edge_recv.at[0], x_up),
        remote(edge_out, edge_in.at[1], edge_send.at[1], edge_recv.at[1], x_down),
    ]
    for stride in strides_of(CELLS)[1:]:
        reduce_links(links, ghost, solved, inverses, CELLS, stride)

    p_slots[core] = packed_links(links[0], ghost[...])
    p_copy = remote(p_slots.at[core], p_slots.at[core], p_send.at[0], p_recv.at[0], partner)

    loads[3].wait()
    for edge in edges:
        edge.wait()
    speed = jnp.broadcast_to(rate[...], (128, W)).T
    for i in range(CELLS):
        own = previous_in[i]
        below = jnp.where(
            lane == 0, pltpu.roll(edge_in[0], (128 - i) % 128, 1), pltpu.roll(own, 1, 1)
        )
        above = jnp.where(
            lane == 127, pltpu.roll(edge_in[1], 127 - W - i, 1), pltpu.roll(own, 127, 1)
        )
        rhs[i] = source_in[i] + speed * (above + below - 2.0 * own)
    rhs_ghost[...] = jnp.zeros_like(rhs_ghost)

    p_copy.wait()
    chain_links(lambda i: p_slots[i], p_links, p_ghost, 2)
    reduce_links(p_links, p_ghost, p_solved, p_inverses, 2, 1)

    payload = packed_links(p_links[0], p_ghost[...])
    z_slots[0, z] = payload[:48]
    z_slots[1, z] = payload[48:]
    z_copies = {
        d: remote(
            z_slots.at[core, z],
            z_slots.at[core, z],
            z_send.at[0, d - 1],
            z_recv.at[0, d - 1],
            z_to[d],
        )
        for d in z_order
    }

    for stride in strides_of(CELLS):
        reduce_rhs(rhs, rhs_ghost, solved, inverses, CELLS, stride)
    p_rslots[core, 0] = rhs[0]
    p_rslots[core, 1] = rhs_ghost[...]
    p_copy = remote(p_rslots.at[core], p_rslots.at[core], p_send.at[1], p_recv.at[1], partner)
    p_copy.wait()
    chain_rhs(lambda i: p_rslots[i, 0], lambda i: p_rslots[i, 1], p_rhs, p_rhs_ghost, 2)
    reduce_rhs(p_rhs, p_rhs_ghost, p_solved, p_inverses, 2, 1)
    z_rslots[0, z] = p_rhs[0]
    z_rslots[1, z] = p_rhs_ghost[...]

    def forward(slots, copies, which):
        passed = []
        for d in z_arrive:
            copies[d].wait_recv()
            behind = lax.rem(z + CHIPS_Z - d, CHIPS_Z)
            passed.append(
                remote(
                    slots.at[core, behind],
                    slots.at[core, behind],
                    f_send.at[which, d - 1],
                    f_recv.at[which, d - 1],
                    partner,
                )
            )
        return passed

    zr_copies = {
        d: remote(
            z_rslots.at[core, z],
            z_rslots.at[core, z],
            z_send.at[1, d - 1],
            z_recv.at[1, d - 1],
            z_to[d],
        )
        for d in z_order
    }
    for copy in forward(z_slots, z_copies, 0):
        copy.wait()
    chain_links(
        lambda i: jnp.concatenate([z_slots[0, i], z_slots[1, i]], axis=0),
        z_links,
        z_ghost,
        CHIPS_Z,
    )
    for stride in strides_of(CHIPS_Z):
        reduce_links(z_links, z_ghost, z_solved, z_inverses, CHIPS_Z, stride)

    y_slots[y] = packed_links(z_links[0], z_ghost[...])
    y_copies = [
        remote(y_slots.at[y], y_slots.at[y], y_send.at[0, d - 1], y_recv.at[0, d - 1], y_to[d])
        for d in y_order
    ]
    for copy in forward(z_rslots, zr_copies, 1):
        copy.wait()
    chain_rhs(lambda i: z_rslots[0, i], lambda i: z_rslots[1, i], z_rhs, z_rhs_ghost, CHIPS_Z)
    for stride in strides_of(CHIPS_Z):
        reduce_rhs(z_rhs, z_rhs_ghost, z_solved, z_inverses, CHIPS_Z, stride)
    y_rslots[y, 0] = z_rhs[0]
    y_rslots[y, 1] = z_rhs_ghost[...]
    yr_copies = [
        remote(
            y_rslots.at[y], y_rslots.at[y], y_send.at[1, d - 1], y_recv.at[1, d - 1], y_to[d]
        )
        for d in y_order
    ]
    for copy in y_copies:
        copy.wait()
    chain_links(lambda i: y_slots[i], y_links, None, CHIPS_Y)
    for stride in strides_of(CHIPS_Y):
        reduce_links(y_links, None, y_solved, y_inverses, CHIPS_Y, stride)
    first = inverse(augmented(y_links[0], None)[None])

    for copy in yr_copies:
        copy.wait()
    chain_rhs(lambda i: y_rslots[i, 0], lambda i: y_rslots[i, 1], y_rhs, None, CHIPS_Y)
    for stride in strides_of(CHIPS_Y):
        reduce_rhs(y_rhs, None, y_solved, y_inverses, CHIPS_Y, stride)
    y_field[0] = dot(first[0][:, :W], y_rhs[0])
    y_field[CHIPS_Y] = jnp.zeros((W, ROWS), jnp.float32)
    expand(y_solved, y_rhs, y_field, CHIPS_Y)
    z_field[0] = y_field[y]
    z_field[CHIPS_Z] = y_field[y + 1]
    expand(z_solved, z_rhs, z_field, CHIPS_Z)
    p_field[0] = z_field[z]
    p_field[2] = z_field[z + 1]
    expand(p_solved, p_rhs, p_field, 2)
    field[0] = p_field[core]
    field[CELLS] = p_field[core + 1]
    expand(solved, rhs, field, CELLS)
    for i in range(CELLS):
        out[i] = field[i]
    for d in z_order:
        z_copies[d].wait_send()
        zr_copies[d].wait_send()


def local(coupling, vertical, source, previous, spread_rate):
    f32 = jnp.float32

    def vmem(*shape):
        return pltpu.VMEM(shape + (128,), f32)

    dma = pltpu.SemaphoreType.DMA

    def level(count):
        return [vmem(count, W), vmem(W), vmem(count, W), vmem(count, W)]

    def level_rhs(count):
        return [vmem(count, W), vmem(W), vmem(count + 1, W)]

    scratch = [
        pltpu.VMEM((CELLS, W, W), f32),
        pltpu.VMEM((CELLS, W, W), f32),
        vmem(CELLS, W),
        vmem(CELLS, W),
        dma((4,)),
        vmem(W),
        vmem(2, W),
        dma((2,)),
        dma((2,)),
    ]
    scratch += level(CELLS) + level_rhs(CELLS)
    scratch += [vmem(2, 96)] + level(2)
    scratch += [vmem(2, 2, W)] + level_rhs(2) + [dma((2,)), dma((2,))]
    scratch += [vmem(2, CHIPS_Z, 48)] + level(CHIPS_Z)
    scratch += [vmem(2, CHIPS_Z, W)] + level_rhs(CHIPS_Z) + [dma((2, CHIPS_Z - 1))] * 4
    scratch += [vmem(CHIPS_Y, 96), vmem(CHIPS_Y, W), vmem(CHIPS_Y, W), vmem(CHIPS_Y, W)]
    scratch += [vmem(CHIPS_Y, 2, W), vmem(CHIPS_Y, W), vmem(CHIPS_Y + 1, W)]
    scratch += [dma((2, CHIPS_Y - 1))] * 2
    anywhere = pl.BlockSpec(memory_space=pl.ANY)
    solved = pl.pallas_call(
        kernel,
        out_shape=jax.ShapeDtypeStruct((CELLS, W, ROWS), f32),
        in_specs=[anywhere] * 4 + [pl.BlockSpec(memory_space=pltpu.VMEM)],
        out_specs=pl.BlockSpec(memory_space=pltpu.VMEM),
        scratch_shapes=scratch,
        compiler_params=pltpu.CompilerParams(
            collective_id=0, has_side_effects=True, vmem_limit_bytes=60 * 1024 * 1024
        ),
        cost_estimate=pl.CostEstimate(
            flops=400_000_000, bytes_accessed=4_000_000, transcendentals=0
        ),
    )(
        coupling,
        vertical,
        jnp.swapaxes(source, 1, 2),
        jnp.swapaxes(previous, 1, 2),
        spread_rate.reshape(1, W),
    )
    return jnp.swapaxes(solved, 1, 2)


def solution(mesh):
    cells = P("gx", None, None)
    slab = P("gx", "gy", None)
    return jax.shard_map(
        local,
        mesh=mesh,
        in_specs=(cells, cells, slab, slab, P()),
        out_specs=slab,
        check_vma=False,
    )
```

time: 92.8 us -> 63 us (0.68)
  Pallas kernels: 87.3 us -> 60.3 us
  local copies, waits for them, and re-layouts: 5.27 us -> 1.89 us
    pallas_call x1, Pallas kernels: 87.3 us -> 60.3 us  [local(): pl.pallas_call(kernel, out_shape=jax.ShapeDtypeStruct((CELLS, W, ROWS), f...]
    unnamed x10 -> x1, local copies, waits for them, and re-layouts: 4.16 us -> 1.89 us
    pallas_call x1 -> x0, local copies, waits for them, and re-layouts: 1.11 us -> none  [local(): pl.pallas_call(kernel, out_shape=jax.ShapeDtypeStruct((CELLS, ROWS, W), f...]
where the time goes in v2:
time: 63 us; the launch traced here: 62.2 us
  Pallas kernels  60.3 us (96%)
  local copies, waits for them, and re-layouts  1.89 us (3%)
    pallas_call x1, Pallas kernels, local(): pl.pallas_call(kernel, out_shape=jax.ShapeDtypeStruct((CELLS, W, ROWS), f...  60.3 us
    unnamed x1, local copies, waits for them, and re-layouts  1.89 us

profile of v2, /device:TPU:1, one launch (start us, length us, event | category | flops | bytes accessed | tf_op | source)
XLA Modules:
  0.0 62.2 jit_solution(8815310529594881980)
XLA Ops:
  0.0 60.3 %shard_map.55 = f32[16,64,128]{2,1,0:T(8,128)} custom-call(f32[16,64,64]{2,1,0:T(8,128)} %coupling.1, f32[16,64,64]{2,1,0:T(8,128)} %vertical.1, f32[16,64,128]{2,1,0:T(8,128)} %bitcast.5, f32[16,64,128]{2,1,0:T(8,128)} %bitcast.6, f32[1,64]{1,0:T(1,128)} %bitcast.7), custom_call_target="tpu_custom_call" | custom-call | flops 400000000 | bytes 4000000 | tf_op jit(solution)/shard_map/pallas_call | solution.py:399
  60.3 1.9 %copy.7 = f32[16,128,64]{1,2,0:T(8,128)} copy(f32[16,128,64]{1,2,0:T(8,128)} %bitcast.4) | data formatting | bytes 1048576

commit v3 on v2

--- a/solution.py
+++ b/solution.py
@@ -29,45 +29,78 @@
 
 
 def lane_copy(value, lane):
-    return jnp.broadcast_to(lax.slice_in_dim(value, lane, lane + 1, axis=2), value.shape)
-
-
-def inverse(augmented):
-    sub = iota((1, 8, 128), 1)
-
-    def block(_, value):
-        columns = [lane_copy(value, j) for j in range(8)]
-        turned = pltpu.roll(value, 120, 2)
-        top = turned[:, :8]
-        head = [column[:, :8] for column in columns]
-        recip = 1.0 / head[0][:, 0:1]
-        for j in range(8):
-            next_recip = None
-            if j < 7:
-                cross = head[j][:, j + 1 : j + 2] * head[j + 1][:, j : j + 1]
-                next_recip = 1.0 / (head[j + 1][:, j + 1 : j + 2] - cross * recip)
-            row = top[:, j : j + 1] * recip
-            for k in range(j + 1, 8):
-                entry = head[k][:, j : j + 1] * recip
-                head[k] = jnp.where(sub == j, entry, head[k] - head[j] * entry)
-            top = jnp.where(sub == j, row, top - head[j] * row)
-            recip = next_recip
-        terms = [columns[j][:, 8:] * top[:, j : j + 1] for j in range(8)]
-        total = ((terms[0] + terms[1]) + (terms[2] + terms[3])) + (
-            (terms[4] + terms[5]) + (terms[6] + terms[7])
-        )
-        return jnp.concatenate([turned[:, 8:] - total, top], axis=1)
-
-    return lax.fori_loop(0, 8, block, augmented)
-
-
-def augmented(link_excess, left, symmetric=False):
+    return jnp.broadcast_to(value[:, lane : lane + 1], value.shape)
+
+
+def pivot_block(rows, head):
+    count = len(head)
+    sub = iota((count, 128), 0)
+    head = list(head)
+    recip = 1.0 / head[0][0:1]
+    for j in range(count):
+        next_recip = None
+        if j < count - 1:
+            cross = head[j][j + 1 : j + 2] * head[j + 1][j : j + 1]
+            next_recip = 1.0 / (head[j + 1][j + 1 : j + 2] - cross * recip)
+        row = rows[j : j + 1] * recip
+        for k in range(j + 1, count):
+            entry = head[k][j : j + 1] * recip
+            head[k] = jnp.where(sub == j, entry, head[k] - head[j] * entry)
+        rows = jnp.where(sub == j, row, rows - head[j] * row)
+        recip = next_recip
+    return rows
+
+
+def sum_of(terms):
+    while len(terms) > 1:
+        pairs = [terms[i] + terms[i + 1] for i in range(0, len(terms) - 1, 2)]
+        terms = pairs + terms[2 * len(pairs) :]
+    return terms[0]
+
+
+def inverses_of(matrices):
+    alone = len(matrices) == 1
+    size = 16 if alone else 8
+    count = W // size
+    blocks = [[m[size * t : size * (t + 1)] for t in range(count)] for m in matrices]
+    for k in range(count):
+        first = size * k
+        lead = first + W if alone else first
+        tops = [
+            pivot_block(rows[k], [lane_copy(rows[k], lead + j) for j in range(size)])
+            for rows in blocks
+        ]
+        others = [t for t in range(count) if t != k]
+        near = others if alone else [(k + 1) % count]
+        far = [t for t in others if t not in near]
+        for rows, top in zip(blocks, tops):
+            for t in near:
+                rows[t] = rows[t] - sum_of(
+                    [lane_copy(rows[t], lead + j) * top[j : j + 1] for j in range(size)]
+                )
+            if far:
+                parts = [top]
+                if first > 0:
+                    parts = [jnp.zeros((first, 128), jnp.float32)] + parts
+                if first + size < W:
+                    parts = parts + [jnp.zeros((W - size - first, 128), jnp.float32)]
+                taken = dot(
+                    jnp.concatenate([rows[t] for t in far], axis=0)[:, :W],
+                    jnp.concatenate(parts, axis=0),
+                )
+                for at, t in enumerate(far):
+                    rows[t] = rows[t] - taken[size * at : size * (at + 1)]
+            rows[k] = top
+    return [jnp.concatenate(rows, axis=0) for rows in blocks]
+
+
+def augmented(link_excess, left, alone, symmetric=False):
     lane = iota((W, 128), 1)
-    eye = (lane == iota((W, 128), 0) + W).astype(jnp.float32)
+    eye = ((lane & (W - 1)) == iota((W, 128), 0)).astype(jnp.float32)
     value = link_excess + pltpu.roll(link_excess, W, 1)
     if left is not None:
         value = value + (left if symmetric else jnp.concatenate([left, left], axis=0).T[:W])
-    return jnp.where(lane < W, value, eye)
+    return jnp.where((lane >= W) if alone else (lane < W), value, eye)
 
 
 def high_lanes(value):
@@ -84,12 +117,20 @@
 
 def reduce_links(links, ghost, solved, inverses, count, stride, symmetric=False):
     picks = picks_of(stride, count)
-    found = inverse(
-        jnp.stack([augmented(links[i], links[i - stride], symmetric) for i in picks])
+    alone = len(picks) == 1
+    found = inverses_of(
+        [augmented(links[i], links[i - stride], alone, symmetric) for i in picks]
     )
     for at, i in enumerate(picks):
-        inverses[i] = found[at]
-        answer = dot(found[at][:, :W], links[i])
+        if alone:
+            inverses[i] = found[at]
+            answer = dot(found[at][:, :W], links[i])
+        else:
+            inverses[i] = pltpu.roll(found[at], W, 1)
+            answer = dot(
+                found[at],
+                jnp.concatenate([jnp.zeros((W, 128), jnp.float32), links[i]], axis=0),
+            )
         solved[i] = answer
         before = links[i - stride]
         links[i - stride] = high_lanes(before) + dot(before[:, :W], answer)
@@ -221,31 +262,17 @@
         edges_value = jnp.where(lane == i, pltpu.roll(own, i + 1, 1), edges_value)
         edges_value = jnp.where(lane == W + i, pltpu.roll(own, W + i, 1), edges_value)
     edge_out[...] = edges_value
+    for stride in strides_of(CELLS)[1:]:
+        reduce_links(links, ghost, solved, inverses, CELLS, stride)
+
     pl.semaphore_wait(barrier, len(everyone))
     edges = [
         remote(edge_out, edge_in.at[0], edge_send.at[0], edge_recv.at[0], x_up),
         remote(edge_out, edge_in.at[1], edge_send.at[1], edge_recv.at[1], x_down),
     ]
-    for stride in strides_of(CELLS)[1:]:
-        reduce_links(links, ghost, solved, inverses, CELLS, stride)
 
     p_slots[core] = packed_links(links[0], ghost[...])
     p_copy = remote(p_slots.at[core], p_slots.at[core], p_send.at[0], p_recv.at[0], partner)
-
-    loads[3].wait()
-    for edge in edges:
-        edge.wait()
-    speed = jnp.broadcast_to(rate[...], (128, W)).T
-    for i in range(CELLS):
-        own = previous_in[i]
-        below = jnp.where(
-            lane == 0, pltpu.roll(edge_in[0], (128 - i) % 128, 1), pltpu.roll(own, 1, 1)
-        )
-        above = jnp.where(
-            lane == 127, pltpu.roll(edge_in[1], 127 - W - i, 1), pltpu.roll(own, 127, 1)
-        )
-        rhs[i] = source_in[i] + speed * (above + below - 2.0 * own)
-    rhs_ghost[...] = jnp.zeros_like(rhs_ghost)
 
     p_copy.wait()
     chain_links(lambda i: p_slots[i], p_links, p_ghost, 2)
@@ -264,6 +291,21 @@
         )
         for d in z_order
     }
+
+    loads[3].wait()
+    for edge in edges:
+        edge.wait()
+    speed = jnp.broadcast_to(rate[...], (128, W)).T
+    for i in range(CELLS):
+        own = previous_in[i]
+        below = jnp.where(
+            lane == 0, pltpu.roll(edge_in[0], (128 - i) % 128, 1), pltpu.roll(own, 1, 1)
+        )
+        above = jnp.where(
+            lane == 127, pltpu.roll(edge_in[1], 127 - W - i, 1), pltpu.roll(own, 127, 1)
+        )
+        rhs[i] = source_in[i] + speed * (above + below - 2.0 * own)
+    rhs_ghost[...] = jnp.zeros_like(rhs_ghost)
 
     for stride in strides_of(CELLS):
         reduce_rhs(rhs, rhs_ghost, solved, inverses, CELLS, stride)
@@ -292,6 +334,7 @@
             )
         return passed
 
+    z_passed = forward(z_slots, z_copies, 0)
     zr_copies = {
         d: remote(
             z_rslots.at[core, z],
@@ -302,7 +345,7 @@
         )
         for d in z_order
     }
-    for copy in forward(z_slots, z_copies, 0):
+    for copy in z_passed:
         copy.wait()
     chain_links(
         lambda i: jnp.concatenate([z_slots[0, i], z_slots[1, i]], axis=0),
@@ -336,7 +379,7 @@
     chain_links(lambda i: y_slots[i], y_links, None, CHIPS_Y)
     for stride in strides_of(CHIPS_Y):
         reduce_links(y_links, None, y_solved, y_inverses, CHIPS_Y, stride)
-    first = inverse(augmented(y_links[0], None)[None])
+    first = inverses_of([augmented(y_links[0], None, True)])
 
     for copy in yr_copies:
         copy.wait()

time: 63 us -> 54.4 us (0.86)
  Pallas kernels: 60.3 us -> 51.7 us
    pallas_call x1, Pallas kernels: 60.3 us -> 51.7 us  [local(): pl.pallas_call(kernel, out_shape=jax.ShapeDtypeStruct((CELLS, W, ROWS), f...]
where the time goes in v3:
time: 54.4 us; the launch traced here: 53.6 us
  Pallas kernels  51.7 us (95%)
  local copies, waits for them, and re-layouts  1.89 us (3%)
    pallas_call x1, Pallas kernels, local(): pl.pallas_call(kernel, out_shape=jax.ShapeDtypeStruct((CELLS, W, ROWS), f...  51.7 us
    unnamed x1, local copies, waits for them, and re-layouts  1.89 us

profile of v3, /device:TPU:1, one launch (start us, length us, event | category | flops | bytes accessed | tf_op | source)
XLA Modules:
  0.0 53.6 jit_solution(3311354601377498153)
XLA Ops:
  0.0 51.7 %shard_map.55 = f32[16,64,128]{2,1,0:T(8,128)} custom-call(f32[16,64,64]{2,1,0:T(8,128)} %coupling.1, f32[16,64,64]{2,1,0:T(8,128)} %vertical.1, f32[16,64,128]{2,1,0:T(8,128)} %bitcast.5, f32[16,64,128]{2,1,0:T(8,128)} %bitcast.6, f32[1,64]{1,0:T(1,128)} %bitcast.7), custom_call_target="tpu_custom_call" | custom-call | flops 400000000 | bytes 4000000 | tf_op jit(solution)/shard_map/pallas_call | solution.py:442
  51.7 1.9 %copy.7 = f32[16,128,64]{1,2,0:T(8,128)} copy(f32[16,128,64]{1,2,0:T(8,128)} %bitcast.4) | data formatting | bytes 1048576

commit v4 on v3

--- a/solution.py
+++ b/solution.py
@@ -160,6 +160,17 @@
             field[i] = rhs[i] + before + dot(solved[i], change)
 
 
+def expand_maps(solved, rhs, maps, count):
+    for stride in reversed(strides_of(count)):
+        for i in picks_of(stride, count):
+            before = jnp.concatenate([maps[i - stride, 0], maps[i - stride, 1]], axis=1)
+            after = jnp.concatenate([maps[i + stride, 0], maps[i + stride, 1]], axis=1)
+            change = jnp.concatenate([after - before, -before], axis=0)
+            found = before + dot(solved[i], change)
+            maps[i, 0] = found[:, :128]
+            maps[i, 1] = found[:, 128:] + rhs[i]
+
+
 def packed_links(link_excess, ghost):
     low = pltpu.roll(ghost[: W // 2], W, 1)
     return jnp.concatenate([link_excess, low + high_lanes(ghost[W // 2 :])], axis=0)
@@ -192,9 +203,9 @@
     (edge_out, edge_in, edge_send, edge_recv) = scratch[5:9]
     (links, ghost, solved, inverses, rhs, rhs_ghost, field) = scratch[9:16]
     (p_slots, p_links, p_ghost, p_solved, p_inverses) = scratch[16:21]
-    (p_rslots, p_rhs, p_rhs_ghost, p_field, p_send, p_recv) = scratch[21:27]
+    (p_rslots, p_rhs, p_rhs_ghost, p_maps, p_send, p_recv) = scratch[21:27]
     (z_slots, z_links, z_ghost, z_solved, z_inverses) = scratch[27:32]
-    (z_rslots, z_rhs, z_rhs_ghost, z_field, z_send, z_recv, f_send, f_recv) = scratch[32:40]
+    (z_rslots, z_rhs, z_rhs_ghost, z_maps, z_send, z_recv, f_send, f_recv) = scratch[32:40]
     (y_slots, y_links, y_solved, y_inverses) = scratch[40:44]
     (y_rslots, y_rhs, y_field, y_send, y_recv) = scratch[44:49]
 
@@ -255,6 +266,13 @@
     ghost[...] = jnp.zeros_like(ghost)
     reduce_links(links, ghost, solved, inverses, CELLS, 1, True)
 
+    for stride in strides_of(CELLS)[1:]:
+        reduce_links(links, ghost, solved, inverses, CELLS, stride)
+
+    pl.semaphore_wait(barrier, len(everyone))
+    p_slots[core] = packed_links(links[0], ghost[...])
+    p_copy = remote(p_slots.at[core], p_slots.at[core], p_send.at[0], p_recv.at[0], partner)
+
     loads[2].wait()
     edges_value = jnp.zeros((W, 128), jnp.float32)
     for i in range(CELLS):
@@ -262,17 +280,10 @@
         edges_value = jnp.where(lane == i, pltpu.roll(own, i + 1, 1), edges_value)
         edges_value = jnp.where(lane == W + i, pltpu.roll(own, W + i, 1), edges_value)
     edge_out[...] = edges_value
-    for stride in strides_of(CELLS)[1:]:
-        reduce_links(links, ghost, solved, inverses, CELLS, stride)
-
-    pl.semaphore_wait(barrier, len(everyone))
     edges = [
         remote(edge_out, edge_in.at[0], edge_send.at[0], edge_recv.at[0], x_up),
         remote(edge_out, edge_in.at[1], edge_send.at[1], edge_recv.at[1], x_down),
     ]
-
-    p_slots[core] = packed_links(links[0], ghost[...])
-    p_copy = remote(p_slots.at[core], p_slots.at[core], p_send.at[0], p_recv.at[0], partner)
 
     p_copy.wait()
     chain_links(lambda i: p_slots[i], p_links, p_ghost, 2)
@@ -374,29 +385,34 @@
         )
         for d in y_order
     ]
+    spot = (lane & (W - 1)) == iota((W, 128), 0)
+    z_maps[0, 0] = jnp.where(spot & (lane >= W), -1.0, 0.0)
+    z_maps[CHIPS_Z, 0] = jnp.where(spot, jnp.where(lane >= W, -1.0, 1.0), 0.0)
+    z_maps[0, 1] = jnp.zeros((W, ROWS), jnp.float32)
+    z_maps[CHIPS_Z, 1] = jnp.zeros((W, ROWS), jnp.float32)
+    expand_maps(z_solved, z_rhs, z_maps, CHIPS_Z)
+    p_maps[0] = z_maps[z]
+    p_maps[2] = z_maps[z + 1]
+    expand_maps(p_solved, p_rhs, p_maps, 2)
+
     for copy in y_copies:
         copy.wait()
     chain_links(lambda i: y_slots[i], y_links, None, CHIPS_Y)
     for stride in strides_of(CHIPS_Y):
         reduce_links(y_links, None, y_solved, y_inverses, CHIPS_Y, stride)
-    first = inverses_of([augmented(y_links[0], None, True)])
-
     for copy in yr_copies:
         copy.wait()
     chain_rhs(lambda i: y_rslots[i, 0], lambda i: y_rslots[i, 1], y_rhs, None, CHIPS_Y)
     for stride in strides_of(CHIPS_Y):
         reduce_rhs(y_rhs, None, y_solved, y_inverses, CHIPS_Y, stride)
+    first = inverses_of([augmented(y_links[0], None, True)])
     y_field[0] = dot(first[0][:, :W], y_rhs[0])
     y_field[CHIPS_Y] = jnp.zeros((W, ROWS), jnp.float32)
     expand(y_solved, y_rhs, y_field, CHIPS_Y)
-    z_field[0] = y_field[y]
-    z_field[CHIPS_Z] = y_field[y + 1]
-    expand(z_solved, z_rhs, z_field, CHIPS_Z)
-    p_field[0] = z_field[z]
-    p_field[2] = z_field[z + 1]
-    expand(p_solved, p_rhs, p_field, 2)
-    field[0] = p_field[core]
-    field[CELLS] = p_field[core + 1]
+    change = jnp.concatenate([y_field[y + 1] - y_field[y], -y_field[y]], axis=0)
+    ends = dot(jnp.concatenate([p_maps[core, 0], p_maps[core + 1, 0]], axis=0), change)
+    field[0] = ends[:W] + p_maps[core, 1]
+    field[CELLS] = ends[W:] + p_maps[core + 1, 1]
     expand(solved, rhs, field, CELLS)
     for i in range(CELLS):
         out[i] = field[i]
@@ -416,8 +432,8 @@
     def level(count):
         return [vmem(count, W), vmem(W), vmem(count, W), vmem(count, W)]
 
-    def level_rhs(count):
-        return [vmem(count, W), vmem(W), vmem(count + 1, W)]
+    def level_rhs(count, *parts):
+        return [vmem(count, W), vmem(W), vmem(count + 1, *parts, W)]
 
     scratch = [
         pltpu.VMEM((CELLS, W, W), f32),
@@ -432,9 +448,9 @@
     ]
     scratch += level(CELLS) + level_rhs(CELLS)
     scratch += [vmem(2, 96)] + level(2)
-    scratch += [vmem(2, 2, W)] + level_rhs(2) + [dma((2,)), dma((2,))]
+    scratch += [vmem(2, 2, W)] + level_rhs(2, 2) + [dma((2,)), dma((2,))]
     scratch += [vmem(2, CHIPS_Z, 48)] + level(CHIPS_Z)
-    scratch += [vmem(2, CHIPS_Z, W)] + level_rhs(CHIPS_Z) + [dma((2, CHIPS_Z - 1))] * 4
+    scratch += [vmem(2, CHIPS_Z, W)] + level_rhs(CHIPS_Z, 2) + [dma((2, CHIPS_Z - 1))] * 4
     scratch += [vmem(CHIPS_Y, 96), vmem(CHIPS_Y, W), vmem(CHIPS_Y, W), vmem(CHIPS_Y, W)]
     scratch += [vmem(CHIPS_Y, 2, W), vmem(CHIPS_Y, W), vmem(CHIPS_Y + 1, W)]
     scratch += [dma((2, CHIPS_Y - 1))] * 2

time: 54.4 us -> 53.2 us (0.978)
  Pallas kernels: 51.7 us -> 50.6 us
    pallas_call x1, Pallas kernels: 51.7 us -> 50.6 us  [local(): pl.pallas_call(kernel, out_shape=jax.ShapeDtypeStruct((CELLS, W, ROWS), f...]
where the time goes in v4:
time: 53.2 us; the launch traced here: 52.5 us
  Pallas kernels  50.6 us (95%)
  local copies, waits for them, and re-layouts  1.89 us (4%)
    pallas_call x1, Pallas kernels, local(): pl.pallas_call(kernel, out_shape=jax.ShapeDtypeStruct((CELLS, W, ROWS), f...  50.6 us
    unnamed x1, local copies, waits for them, and re-layouts  1.89 us

profile of v4, /device:TPU:1, one launch (start us, length us, event | category | flops | bytes accessed | tf_op | source)
XLA Modules:
  0.0 52.5 jit_solution(6038458846428694621)
XLA Ops:
  0.0 50.6 %shard_map.55 = f32[16,64,128]{2,1,0:T(8,128)} custom-call(f32[16,64,64]{2,1,0:T(8,128)} %coupling.1, f32[16,64,64]{2,1,0:T(8,128)} %vertical.1, f32[16,64,128]{2,1,0:T(8,128)} %bitcast.5, f32[16,64,128]{2,1,0:T(8,128)} %bitcast.6, f32[1,64]{1,0:T(1,128)} %bitcast.7), custom_call_target="tpu_custom_call" | custom-call | flops 400000000 | bytes 4000000 | tf_op jit(solution)/shard_map/pallas_call | solution.py:458
  50.6 1.9 %copy.7 = f32[16,128,64]{1,2,0:T(8,128)} copy(f32[16,128,64]{1,2,0:T(8,128)} %bitcast.4) | data formatting | bytes 1048576
